TPU v7x, 128 devices: a whole 4x4x4 slice. The times are simulated.
128 devices in a mesh: pts: 64 (over z, y, x), head: 2 (over core).
Axes of the slice: x: 4, y: 4, z: 4, core: 2. Of those that a mesh axis runs over, the one named last changes fastest.
Arguments:
- points: bfloat16 [64, 262144], P(None, 'pts'), may hold values from -64 to 64
- counts: int32 [64], P('pts'), may hold values from 1 to 4096, 196608 in all
- latents_init: bfloat16 [512, 768], P('head'), may hold values from -6 to 6
- enc_key_w: bfloat16 [64, 768], replicated, may hold values from -0.75 to 0.75
- enc_val_w: bfloat16 [64, 768], replicated, may hold values from -0.75 to 0.75
- lat_weights: bfloat16 [7, 768, 768], P(None, 'head'), may hold values from -0.21875 to 0.21875
- up_w: bfloat16 [768, 3072], P(None, 'head'), may hold values from -0.21875 to 0.21875
- down_w: bfloat16 [3072, 768], P('head'), may hold values from -0.109375 to 0.109375
- query_w: bfloat16 [64, 768], replicated, may hold values from -0.75 to 0.75
- class_w: bfloat16 [768, 16], replicated, may hold values from -0.21875 to 0.21875
Outputs:
- logits: float32 [16, 262144], P(None, ('pts', 'head'))
Inputs may be any that keep to these rules, and one draw needn't show every extreme that they name: `counts`: every shard has at least one live point and one shard has exactly 4096.
All inputs are finite; a program needn't handle non-finite values.
Results may differ from a plain program's by a relative error of at most 0.025.
Values may be sent and summed in bfloat16 or wider, within the bound.
No kernel may reach another device: no remote copies, remote signals or barrier semaphores. Data moves between devices by JAX's collectives and lax.ppermute only.
A program may use at most 192 MiB of HBM per device.

v0:
```python
import math

import jax
import jax.numpy as jnp
from jax import lax
from jax.experimental import pallas as pl
from jax.experimental.pallas import tpu as pltpu
from jax.sharding import PartitionSpec as P

HEADS = 12
HSIZE = 64
WIDTH = HEADS * HSIZE
PAIRS = HEADS // 2
HALF = WIDTH // 2
KEY, VAL, QUERY, CLASS = 0, 64, 128, 192
OWNERS = 64
GROUPS = 32
LOG2_SCALE = HSIZE ** -0.5 * math.log2(math.e)
SAFE = 64.0
DEAD = -1e30

f32 = jnp.float32
bf16 = jnp.bfloat16
NT = (((1,), (1,)), ((), ()))
NN = (((1,), (0,)), ((), ()))


def dot(a, b, dims=NN):
    return lax.dot_general(a, b, dims, preferred_element_type=f32)


def norm(v):
    mean = jnp.mean(v, axis=-1, keepdims=True)
    cent = v - mean
    var = jnp.mean(cent * cent, axis=-1, keepdims=True)
    return cent * lax.rsqrt(var + 1e-05)


def split3(v):
    hi = v.astype(bf16).astype(f32)
    mid = (v - hi).astype(bf16).astype(f32)
    lo = (v - hi - mid).astype(bf16).astype(f32)
    return hi, mid, lo


def lanes(shape):
    return lax.broadcasted_iota(jnp.int32, shape, len(shape) - 1)


def block_diag(pair):
    lane = lanes(pair.shape)
    zero = jnp.zeros_like(pair)
    return jnp.concatenate([jnp.where(lane < 64, pair, zero), jnp.where(lane >= 64, pair, zero)], axis=0)


def vmem():
    return pl.BlockSpec(memory_space=pltpu.VMEM)


def smem():
    return pl.BlockSpec(memory_space=pltpu.SMEM)


def anywhere():
    return pl.BlockSpec(memory_space=pl.ANY)


def shape(dims, dtype=bf16):
    return jax.ShapeDtypeStruct(dims, dtype)


def params(mib=28):
    return pltpu.CompilerParams(vmem_limit_bytes=mib << 20)


def cost(flops, size, exps=0):
    return pl.CostEstimate(flops=flops, bytes_accessed=size, transcendentals=exps)


def prepare_kernel(count_ref, pts_ref, pack_ref, paug, pvt, normed, pn_ref):
    slots = pts_ref.shape[1]
    count = count_ref[0]
    sub = lax.broadcasted_iota(jnp.int32, (64, slots), 0)
    col = lanes((64, slots))
    ext = jnp.where(sub < 3, 1.0, jnp.where((sub == 3) & (col >= count), DEAD, 0.0))
    paug[0:64, :] = pts_ref[...]
    paug[64:128, :] = ext.astype(bf16)
    for i in range(slots // 128):
        blk = pts_ref[:, i * 128 : (i + 1) * 128].astype(f32)
        full = jnp.concatenate([blk, jnp.ones((64, 128), f32)], axis=0)
        pvt[i * 128 : (i + 1) * 128, :] = full.T.astype(bf16)
    normed[...] = norm(pack_ref[HALF:, :].astype(f32)).astype(bf16)
    pall = pts_ref[...].astype(f32)
    pn_ref[0] = jnp.max(jnp.sum(pall * pall, axis=0, keepdims=True))


def prepare(count, points, pack):
    slots = points.shape[1]
    return pl.pallas_call(
        prepare_kernel,
        out_shape=(shape((128, slots)), shape((slots, 128)), shape((pack.shape[0] - HALF, WIDTH)), shape((1,), f32)),
        in_specs=[smem(), vmem(), vmem()],
        out_specs=(vmem(), vmem(), vmem(), smem()),
        compiler_params=params(),
        cost_estimate=cost(0, 6 << 20),
        name="prepare",
    )(count, points, pack)


ROW_TILE = 512
PT_TILE = 512


def encode_kernel(pos_ref, pn_ref, normed, pack_own, pack_oth, small, paug, pvt, out_ref, qf, qaug, acc):
    rows = qaug.shape[0]
    slots = paug.shape[1]

    lo, hi = normed[:, :HALF], normed[:, HALF:]
    first = pos_ref[0] == 0
    equery = dot(jnp.where(first, lo, hi), pack_own[:HALF, :]) + dot(jnp.where(first, hi, lo), pack_oth[:HALF, :])
    equery = equery.astype(bf16)
    lane8 = lanes((GROUPS, 8, 128))
    aug = jnp.where(lane8 == 67, 1.0, 0.0)
    for p in range(PAIRS):
        cols = slice(p * 128, (p + 1) * 128)
        x = dot(equery[:, cols], block_diag(small[KEY : KEY + 64, cols]), NT) * LOG2_SCALE
        x8 = x.reshape(GROUPS, 8, 128)
        y8 = pltpu.roll(x, 64, 1).reshape(GROUPS, 8, 128)
        s, q = p // 3, p % 3
        qf[0, :, s, q] = jnp.where(lane8 < 64, x8, aug)
        qf[1, :, s, q] = jnp.where(lane8 < 64, y8, aug)
    qall = qf[...].reshape(rows, 128)
    qaug[...] = qall.astype(bf16)

    sub = lax.broadcasted_iota(jnp.int32, (128, 128), 0)
    sums = dot((qall * qall).astype(bf16), jnp.where(sub < 64, 1.0, 0.0).astype(bf16))
    shifted = jnp.max(sums) * pn_ref[0] > SAFE * SAFE

    @pl.when(shifted)
    def _():
        def tile(t, _):
            base = pl.multiple_of(t * ROW_TILE, ROW_TILE)
            qt = qaug[pl.ds(base, ROW_TILE), :]

            def chunk(j, top):
                start = pl.multiple_of(j * PT_TILE, PT_TILE)
                sc = dot(qt, paug[:, pl.ds(start, PT_TILE)])
                return jnp.maximum(top, jnp.max(sc, axis=1, keepdims=True))

            top = lax.fori_loop(0, slots // PT_TILE, chunk, jnp.full((ROW_TILE, 1), DEAD, f32))
            hi, mid, lo = split3(top)
            lane = lanes((ROW_TILE, 128))
            shift = jnp.where(lane == 64, hi, jnp.where(lane == 65, mid, lo))
            keep = (lane < 64) | (lane > 66)
            qaug[pl.ds(base, ROW_TILE), :] = jnp.where(keep, qt.astype(f32), -shift).astype(bf16)
            return 0

        lax.fori_loop(0, rows // ROW_TILE, tile, 0)

    def tile(t, _):
        base = pl.multiple_of(t * ROW_TILE, ROW_TILE)
        qt = qaug[pl.ds(base, ROW_TILE), :]
        total = jnp.zeros((ROW_TILE, 128), f32)
        chunks = [slice(j * PT_TILE, (j + 1) * PT_TILE) for j in range(slots // PT_TILE)]
        coming = dot(qt, paug[:, chunks[0]])
        for j, cols in enumerate(chunks):
            sc = coming
            if j + 1 < len(chunks):
                coming = dot(qt, paug[:, chunks[j + 1]])
            total = total + dot(jnp.exp2(sc).astype(bf16), pvt[cols, :])
        acc[pl.ds(base, ROW_TILE), :] = total
        return 0

    lax.fori_loop(0, rows // ROW_TILE, tile, 0)

    sums = acc[...].reshape(2, OWNERS, 3, 8, 128)
    turned = pltpu.roll(acc[rows // 2 :, :], 64, 1).reshape(OWNERS, 3, 8, 128)
    lane = lanes((OWNERS, 8, 128))
    parts = [jnp.where(lane < 64, sums[0, :, q], turned[:, q]) for q in range(3)]
    extra = jnp.zeros((OWNERS, 8, 128), f32)
    for e in range(2):
        for q in range(3):
            extra = jnp.where(lane == 64 + 3 * e + q, sums[e, :, q], extra)
    out_ref[...] = jnp.concatenate(parts + [extra], axis=1).astype(bf16)

    @pl.when(shifted)
    def _():
        shifts = -qaug[...].astype(f32).reshape(2, OWNERS, 3, 8, 128)
        more = extra
        for e in range(2):
            for q in range(3):
                for k in range(3):
                    one = shifts[e, :, q, :, 64 + k : 65 + k]
                    more = jnp.where(lane == 72 + 8 * k + 3 * e + q, one, more)
        out_ref[...] = jnp.concatenate(parts + [more], axis=1).astype(bf16)


def encode(pos, pn, normed, pack_own, pack_oth, small, paug, pvt):
    slots = paug.shape[1]
    rows = normed.shape[0] * HEADS
    return pl.pallas_call(
        encode_kernel,
        out_shape=shape((OWNERS, 32, 128)),
        in_specs=[smem(), smem()] + [vmem()] * 6,
        out_specs=vmem(),
        scratch_shapes=[
            pltpu.VMEM((2, GROUPS, 2, 3, 8, 128), f32),
            pltpu.VMEM((rows, 128), bf16),
            pltpu.VMEM((rows, 128), f32),
        ],
        compiler_params=params(),
        cost_estimate=cost(rows * slots * 1024, 6 << 20, rows * slots),
        name="encode",
    )(pos, pn, normed, pack_own, pack_oth, small, paug, pvt)


def merge_kernel(x_ref, out_ref, both):
    x = x_ref[...].astype(f32)
    ext = x[:, 24:32, :]
    lane = lanes(ext.shape)
    flag = jnp.max(jnp.where((lane >= 72) & (lane < 96), jnp.abs(ext), 0.0))
    both[...] = jnp.sum(x, axis=0)

    @pl.when(flag > 0.0)
    def _():
        shift = pltpu.roll(ext, 128 - 8, 2) + pltpu.roll(ext, 128 - 16, 2) + pltpu.roll(ext, 128 - 24, 2)
        wt = jnp.exp2(shift - jnp.max(shift, axis=0, keepdims=True))
        wt = jnp.where((lane >= 64) & (lane < 70), wt, 0.0)
        both[24:32, :] = jnp.sum(ext * wt, axis=0)
        for q in range(3):
            fac = jnp.where(lane < 64, wt[:, :, 64 + q : 65 + q], wt[:, :, 67 + q : 68 + q])
            both[q * 8 : (q + 1) * 8, :] = jnp.sum(x[:, q * 8 : (q + 1) * 8, :] * fac, axis=0)

    low = lanes((8, 128)) < 64
    parts = []
    for q in range(3):
        tot = jnp.where(low, both[24:32, 64 + q : 65 + q], both[24:32, 67 + q : 68 + q])
        parts.append(both[q * 8 : (q + 1) * 8, :] / tot)
    mean = jnp.concatenate(parts, axis=0).astype(bf16)
    for k in range(out_ref.shape[0]):
        out_ref[k] = mean


def merge(parts, copies):
    return pl.pallas_call(
        merge_kernel,
        out_shape=shape((copies, 24, 128)),
        in_specs=[vmem()],
        out_specs=vmem(),
        scratch_shapes=[pltpu.VMEM((32, 128), f32)],
        compiler_params=params(),
        cost_estimate=cost(0, 1 << 20),
        name="merge",
    )(parts)


def latent_kernel(
    pos_ref, g_own, g_oth, pack_own, pack_oth, small,
    wl_own, wl_oth, up_own, up_oth, down_own, down_oth,
    at_ref, b_ref,
    enc, mix,
):
    rows = mix.shape[0]
    head = pos_ref[0]
    first = head == 0
    for k, (g, pack) in enumerate(((g_own, pack_own), (g_oth, pack_oth))):
        mean = g[...].astype(f32).reshape(GROUPS, 2, 3, 8, 128)
        for p in range(PAIRS):
            cols = slice(p * 128, (p + 1) * 128)
            part = mean[:, p // 3, p % 3].reshape(rows, 128).astype(bf16)
            val = dot(part, block_diag(small[VAL : VAL + 64, cols]))
            enc[k * rows : (k + 1) * rows, cols] = (pack[HALF:, cols].astype(f32) + val).astype(bf16)
    block_in = norm(enc[...].astype(f32)).astype(bf16)

    def proj(x, i):
        lo, hi = x[:, :HALF], x[:, HALF:]
        return dot(jnp.where(first, lo, hi), wl_own[i]) + dot(jnp.where(first, hi, lo), wl_oth[i])

    keys = proj(block_in, 2).astype(bf16)
    vals = proj(block_in, 3).astype(bf16)
    query = proj(block_in[:rows], 1).astype(bf16)
    ones = jnp.ones((2 * rows, 128), bf16)
    low = lanes((rows, 128)) < 64
    zero = jnp.zeros((rows, 128), bf16)
    for p in range(PAIRS):
        cols = slice(p * 128, (p + 1) * 128)
        qp = query[:, cols]
        both = jnp.concatenate([jnp.where(low, qp, zero), jnp.where(low, zero, qp)], axis=0)
        sc = dot(both, keys[:, cols], NT) * LOG2_SCALE
        ex = jnp.exp2(sc - jnp.max(sc, axis=-1, keepdims=True)).astype(bf16)
        res = dot(ex, jnp.concatenate([vals[:, cols], ones], axis=1))
        res = res[:, :128] / res[:, 128:]
        mix[:, cols] = jnp.where(low, res[:rows], res[rows:]).astype(bf16)
    latent2 = enc[:rows].astype(f32) + proj(mix[...], 4)
    mlp_in = norm(latent2).astype(bf16)
    hidden = []
    for up in (up_own, up_oth):
        x = dot(mlp_in, up[...])
        hid = 0.5 * x * (1.0 + jnp.tanh(math.sqrt(2.0 / math.pi) * (x + 0.044715 * (x * x * x))))
        hidden.append(hid.astype(bf16))
    latents_out = (latent2 + dot(hidden[0], down_own[...]) + dot(hidden[1], down_oth[...])).astype(bf16)
    dec_in = norm(latents_out.astype(f32)).astype(bf16)
    dkeys = proj(dec_in, 5).astype(bf16)
    for p in range(PAIRS):
        cols = slice(p * 128, (p + 1) * 128)
        at_ref[cols, :] = (dot(block_diag(small[QUERY : QUERY + 64, cols]), dkeys[:, cols], NT) * LOG2_SCALE).astype(bf16)
    dvals = proj(dec_in, 6).astype(bf16)
    classes = small[CLASS : CLASS + 16, :]
    lane = lanes(classes.shape)
    none = jnp.zeros_like(classes)
    blocks = [jnp.where((lane >= 64 * h) & (lane < 64 * h + 64), classes, none) for h in range(16)]
    b_ref[...] = dot(dvals, jnp.concatenate(blocks, axis=0), NT).astype(bf16)


def latent_block(pos, g_own, g_oth, pack_own, pack_oth, small, weights):
    rows = pack_own.shape[0] - HALF
    return pl.pallas_call(
        latent_kernel,
        out_shape=(shape((WIDTH, rows)), shape((rows, 256))),
        in_specs=[smem()] + [vmem()] * 11,
        out_specs=(vmem(), vmem()),
        scratch_shapes=[
            pltpu.VMEM((2 * rows, WIDTH), bf16),
            pltpu.VMEM((rows, WIDTH), bf16),
        ],
        compiler_params=params(),
        cost_estimate=cost(6 << 30, 20 << 20, 3 << 20),
        name="latent_block",
    )(pos, g_own, g_oth, pack_own, pack_oth, small, *weights)


DEC_TILE = 512


def decode_kernel(pos_ref, pn_ref, pts_ref, at_own, at_oth, b_own, b_oth, out_ref, pt, amat, bmat):
    share = out_ref.shape[1]
    rows = b_own.shape[0]
    for i in range(share // 128):
        start = pl.multiple_of(pos_ref[0] * share + i * 128, 128)
        blk = pts_ref[:, pl.ds(start, 128)].astype(f32)
        full = jnp.concatenate([blk, jnp.zeros((64, 128), f32)], axis=0)
        pt[i * 128 : (i + 1) * 128, :] = full.T.astype(bf16)
    sub = lax.broadcasted_iota(jnp.int32, (64, 2 * rows), 0)
    lane = lanes((rows, 128))
    worst = jnp.zeros((1, rows), f32)
    for h in range(HEADS):
        amat[h, 64:128, :] = jnp.where((sub >= 3 * h) & (sub < 3 * h + 3), 1.0, 0.0).astype(bf16)
        for k, (a, b) in enumerate(((at_own, b_own), (at_oth, b_oth))):
            part = a[h * 64 : (h + 1) * 64, :]
            amat[h, 0:64, k * rows : (k + 1) * rows] = part
            part = part.astype(f32)
            worst = jnp.maximum(worst, jnp.sum(part * part, axis=0, keepdims=True))
            g = h // 8
            own = (lane >= 16 * (h % 8)) & (lane < 16 * (h % 8) + 16)
            vals = b[:, g * 128 : (g + 1) * 128]
            bmat[h, k * rows : (k + 1) * rows, 0:128] = jnp.where(own, vals, jnp.zeros_like(vals))
            bmat[h, k * rows : (k + 1) * rows, 128:256] = jnp.ones((rows, 128), bf16)
    lane = lanes((DEC_TILE, 128))

    @pl.when(jnp.max(worst) * pn_ref[0] > SAFE * SAFE)
    def _():
        def block(j, _):
            at = pl.ds(pl.multiple_of(j * DEC_TILE, DEC_TILE), DEC_TILE)
            pts = pt[at, :]
            new = pts.astype(f32)
            for h in range(HEADS):
                top = jnp.max(dot(pts, amat[h]), axis=1, keepdims=True)
                for k, part in enumerate(split3(top)):
                    new = jnp.where(lane == 64 + 3 * h + k, -part, new)
            pt[at, :] = new.astype(bf16)
            return 0

        lax.fori_loop(0, share // DEC_TILE, block, 0)

    def block(j, _):
        at = pl.ds(pl.multiple_of(j * DEC_TILE, DEC_TILE), DEC_TILE)
        pts = pt[at, :]
        total = jnp.zeros((DEC_TILE, 128), f32)
        coming = dot(pts, amat[0])
        for h in range(HEADS):
            sc = coming
            if h + 1 < HEADS:
                coming = dot(pts, amat[h + 1])
            res = dot(jnp.exp2(sc).astype(bf16), bmat[h])
            total = total + res[:, :128] / res[:, 128:]
        for turn in (64, 32, 16):
            total = total + pltpu.roll(total, turn, 1)
        out_ref[:, at] = total.T[0:16, :]
        return 0

    lax.fori_loop(0, share // DEC_TILE, block, 0)


def decode(pos, pn, points, at_own, at_oth, b_own, b_oth):
    rows = b_own.shape[0]
    share = points.shape[1] // 2
    return pl.pallas_call(
        decode_kernel,
        out_shape=shape((16, share), f32),
        in_specs=[smem(), smem()] + [vmem()] * 5,
        out_specs=vmem(),
        scratch_shapes=[
            pltpu.VMEM((share, 128), bf16),
            pltpu.VMEM((HEADS, 128, 2 * rows), bf16),
            pltpu.VMEM((HEADS, 2 * rows, 256), bf16),
        ],
        compiler_params=params(),
        cost_estimate=cost(3 << 32, 8 << 20, 12 << 20),
        name="decode",
    )(pos, pn, points, at_own, at_oth, b_own, b_oth)


def per_device(
    points, counts, latents_init, enc_key_w, enc_val_w, lat_weights, up_w, down_w, query_w, class_w
):
    swap = [(0, 1), (1, 0)]

    def other(x):
        return lax.ppermute(x, "head", swap)

    pos = lax.axis_index("head").astype(jnp.int32).reshape(1)
    pack_own = jnp.concatenate([lat_weights[0], latents_init], axis=0)
    pack_oth = other(pack_own)
    small = jnp.concatenate([enc_key_w, enc_val_w, query_w, class_w.T], axis=0)
    paug, pvt, normed, pn = prepare(counts, points, pack_own)
    (pn, pack_oth), late = lax.optimization_barrier(((pn, pack_oth), (lat_weights, up_w, down_w)))
    wl_oth, up_oth, down_oth = [other(w) for w in late]
    part = encode(pos, pn, normed, pack_own, pack_oth, small, paug, pvt)

    parts = lax.all_to_all(part, "pts", 0, 0)
    g_own = lax.all_to_all(merge(parts, OWNERS), "pts", 0, 0)
    g_oth = other(g_own)

    weights = (lat_weights, wl_oth, up_w, up_oth, down_w, down_oth)
    at_own, b_own = latent_block(pos, g_own, g_oth, pack_own, pack_oth, small, weights)
    return decode(pos, pn, points, at_own, other(at_own), b_own, other(b_own))


def solution(mesh):
    placed = (
        P(None, "pts"),
        P("pts"),
        P("head", None),
        P(),
        P(),
        P(None, "head", None),
        P(None, "head"),
        P("head", None),
        P(),
        P(),
    )
    return jax.shard_map(
        per_device, mesh=mesh, in_specs=placed, out_specs=P(None, ("pts", "head")), check_vma=False
    )
```

profile of v0, /device:TPU:1, one launch (start us, length us, event | category | flops | bytes accessed | tf_op | source)
XLA Modules:
  0.0 134.0 jit_solution(2590779629964457951)
XLA Ops:
  0.0 1.2 slice_bitcast_fusion
  1.2 1.1 pad_maximum_fusion.pack_ref.pack_own
  2.2 1.5 %collective-permute-start = (bf16[640,768]{1,0:T(8,128)(2,1)S(1)}, bf16[640,768]{1,0:T(8,128)(2,1)S(1)}, u32[]{:S(2)}, u32[]{:S(2)}) collective-permute-start(bf16[640,768]{1,0:T(8,128)(2,1)S(1)} %pad_maximum_fusion.pack_ref.pack_own), channel_id=1, source_target_pairs={{0,1},{1,0},{2,3},{3,2},{4,5},{5,4},{6,7},{7,6},{8,9},{9,8},{10,11... | collective-permute-start | bytes 2949128 | tf_op jit(solution)/shard_map/ppermute | solution.py:419
  4.4 0.0 copy-done
  4.4 1.1 prepare.1
  5.5 0.0 copy-start.3
  5.5 1.0 copy-done.3
  6.5 0.8 copy-done.5
  7.3 0.0 collective-permute-done.pack_oth
  7.3 0.0 collective-permute-start.2
  7.3 1.0 pad_maximum_fusion.1.small
  8.3 0.6 collective-permute-start.3
  8.9 0.1 collective-permute-start.4
  9.0 1.2 copy-done.4
  10.2 1.0 copy-done.6
  11.2 37.7 %encode.1 = bf16[64,32,128]{2,1,0:T(8,128)(2,1)S(1)} custom-call(s32[1]{0:T(128)} %bitcast.pos_ref, f32[1]{0:T(128)} %get-tuple-element.17.pn_ref, bf16[256,768]{1,0:T(8,128)(2,1)S(1)} %copy-done.6, bf16[640,768]{1,0:T(8,128)(2,1)S(1)} %pad_maximum_fusion.pack_ref.pack_own, bf16[640,768]{1,0:T(8,128)(2,1)S(1)} %collective-permute-done.pack_oth, ...), custom_call_target="tpu_custom_call" | custom-call | flops 12884901888 | bytes 6291456 | tf_op jit(solution)/shard_map/encode/pallas_call | solution.py:201
  48.9 0.0 copy-start.1
  48.9 23.5 %all_to_all.10.x_ref = bf16[64,32,128]{2,1,0:T(8,128)(2,1)S(1)} all-to-all(bf16[64,32,128]{2,1,0:T(8,128)(2,1)S(1)} %encode.1), channel_id=1, replica_groups=mesh['pts'=64,'head'=2] {'pts'}, dimensions={0} | all-to-all | bytes 1048576 | tf_op jit(solution)/shard_map/all_to_all | solution.py:430
  72.5 1.0 merge.1
  73.4 14.5 %all_to_all.11.g_own = bf16[64,24,128]{2,1,0:T(8,128)(2,1)S(1)} all-to-all(bf16[64,24,128]{2,1,0:T(8,128)(2,1)S(1)} %merge.1), channel_id=1, replica_groups=mesh['pts'=64,'head'=2] {'pts'}, dimensions={0} | all-to-all | bytes 786432 | tf_op jit(solution)/shard_map/all_to_all | solution.py:431
  87.9 3.3 %collective-permute-start.1 = (bf16[64,24,128]{2,1,0:T(8,128)(2,1)S(1)}, bf16[64,24,128]{2,1,0:T(8,128)(2,1)S(1)}, u32[]{:S(2)}, u32[]{:S(2)}) collective-permute-start(bf16[64,24,128]{2,1,0:T(8,128)(2,1)S(1)} %all_to_all.11.g_own), channel_id=1, source_target_pairs={{0,1},{1,0},{2,3},{3,2},{4,5},{5,4},{6,7},{7,6},{8,9},{9,8},{10,11... | collective-permute-start | bytes 1179656 | tf_op jit(solution)/shard_map/ppermute | solution.py:419
  91.2 1.3 %collective-permute-done.1.g_oth = bf16[64,24,128]{2,1,0:T(8,128)(2,1)S(1)} collective-permute-done((bf16[64,24,128]{2,1,0:T(8,128)(2,1)S(1)}, bf16[64,24,128]{2,1,0:T(8,128)(2,1)S(1)}, u32[]{:S(2)}, u32[]{:S(2)}) %collective-permute-start.1) | collective-permute-done | bytes 393248 | tf_op jit(solution)/shard_map/ppermute | solution.py:419
  92.5 0.0 collective-permute-done.3.up_oth
  92.5 0.0 collective-permute-done.4.down_oth
  92.5 0.0 collective-permute-done.2.wl_oth
  92.5 0.0 copy-done.2
  92.6 14.3 %latent_block.1 = (bf16[768,256]{1,0:T(8,128)(2,1)S(1)}, bf16[256,256]{1,0:T(8,128)(2,1)S(1)}) custom-call(s32[1]{0:T(128)} %bitcast.pos_ref, bf16[64,24,128]{2,1,0:T(8,128)(2,1)S(1)} %all_to_all.11.g_own, bf16[64,24,128]{2,1,0:T(8,128)(2,1)S(1)} %collective-permute-done.1.g_oth, bf16[640,768]{1,0:T(8,128)(2,1)S(1)} %pad_maximum_fusion.pack_ref.pack_own, ...), custom_call_target="tpu_custom_call" | custom-call | flops 6442450944 | bytes 20971520 | tf_op jit(solution)/shard_map/latent_block/pallas_call | solution.py:317
  106.9 0.5 collective-permute-start.5
  107.3 0.1 collective-permute-start.6
  107.5 1.4 %collective-permute-done.6.b_oth = bf16[256,256]{1,0:T(8,128)(2,1)S(1)} collective-permute-done((bf16[256,256]{1,0:T(8,128)(2,1)S(1)}, bf16[256,256]{1,0:T(8,128)(2,1)S(1)}, u32[]{:S(2)}, u32[]{:S(2)}) %collective-permute-start.6) | collective-permute-done | bytes 131104 | tf_op jit(solution)/shard_map/ppermute | solution.py:419
  108.9 0.0 collective-permute-done.5.at_oth
  108.9 25.1 %decode.1 = f32[16,2048]{1,0:T(8,128)} custom-call(s32[1]{0:T(128)} %bitcast.pos_ref, f32[1]{0:T(128)} %get-tuple-element.17.pn_ref, bf16[64,4096]{1,0:T(8,128)(2,1)S(1)} %copy-done, bf16[768,256]{1,0:T(8,128)(2,1)S(1)} %get-tuple-element.25.at_own, bf16[768,256]{1,0:T(8,128)(2,1)S(1)} %collective-permute-done.5.at_oth, ...), custom_call_target="tpu_custom_call" | custom-call | flops 12884901888 | bytes 8388608 | tf_op jit(solution)/shard_map/decode/pallas_call | solution.py:397
  (6 shorter events, 0.0 us)
Async XLA Ops:
  0.0 4.4 %copy-start = (bf16[64,4096]{1,0:T(8,128)(2,1)S(1)}, bf16[64,4096]{1,0:T(8,128)(2,1)}, u32[]{:S(2)}) copy-start(bf16[64,4096]{1,0:T(8,128)(2,1)} %pts_ref.3) | copy-start | bytes 1572868
  2.2 5.1 %collective-permute-start = (bf16[640,768]{1,0:T(8,128)(2,1)S(1)}, bf16[640,768]{1,0:T(8,128)(2,1)S(1)}, u32[]{:S(2)}, u32[]{:S(2)}) collective-permute-start(bf16[640,768]{1,0:T(8,128)(2,1)S(1)} %pad_maximum_fusion.pack_ref.pack_own), channel_id=1, source_target_pairs={{0,1},{1,0},{2,3},{3,2},{4,5},{5,4},{6,7},{7,6},{8,9},{9,8},{10,11... | collective-permute-start | bytes 2949128 | tf_op jit(solution)/shard_map/ppermute | solution.py:419
  5.5 1.0 copy-start.3
  6.5 0.8 copy-start.5
  7.3 85.2 %collective-permute-start.2 = (bf16[7,384,768]{2,1,0:T(8,128)(2,1)}, bf16[7,384,768]{2,1,0:T(8,128)(2,1)}, u32[]{:S(2)}, u32[]{:S(2)}) collective-permute-start(bf16[7,384,768]{2,1,0:T(8,128)(2,1)} %wl_own.1), channel_id=1, source_target_pairs={{0,1},{1,0},{2,3},{3,2},{4,5},{5,4},{6,7},{7,6},{8,9},{9,8},{10,11... | collective-permute-start | bytes 12386312 | tf_op jit(solution)/shard_map/ppermute | solution.py:419
  8.3 84.2 %collective-permute-start.3 = (bf16[768,1536]{1,0:T(8,128)(2,1)}, bf16[768,1536]{1,0:T(8,128)(2,1)S(1)}, u32[]{:S(2)}, u32[]{:S(2)}) collective-permute-start(bf16[768,1536]{1,0:T(8,128)(2,1)} %up_own.1), channel_id=1, source_target_pairs={{0,1},{1,0},{2,3},{3,2},{4,5},{5,4},{6,7},{7,6},{8,9},{9,8},{10,11... | collective-permute-start | bytes 7077896 | tf_op jit(solution)/shard_map/ppermute | solution.py:419
  8.9 83.6 %collective-permute-start.4 = (bf16[1536,768]{1,0:T(8,128)(2,1)}, bf16[1536,768]{1,0:T(8,128)(2,1)S(1)}, u32[]{:S(2)}, u32[]{:S(2)}) collective-permute-start(bf16[1536,768]{1,0:T(8,128)(2,1)} %down_own.1), channel_id=1, source_target_pairs={{0,1},{1,0},{2,3},{3,2},{4,5},{5,4},{6,7},{7,6},{8,9},{9,8},{10,11... | collective-permute-start | bytes 7077896 | tf_op jit(solution)/shard_map/ppermute | solution.py:419
  9.0 1.2 copy-start.4
  10.2 1.0 copy-start.6
  11.2 81.3 %copy-start.2 = (bf16[1536,768]{1,0:T(8,128)(2,1)S(1)}, bf16[1536,768]{1,0:T(8,128)(2,1)}, u32[]{:S(2)}) copy-start(bf16[1536,768]{1,0:T(8,128)(2,1)} %down_own.1) | copy-start | bytes 7077892
  48.9 43.6 %copy-start.1 = (bf16[768,1536]{1,0:T(8,128)(2,1)S(1)}, bf16[768,1536]{1,0:T(8,128)(2,1)}, u32[]{:S(2)}) copy-start(bf16[768,1536]{1,0:T(8,128)(2,1)} %up_own.1) | copy-start | bytes 7077892
  87.9 4.6 %collective-permute-start.1 = (bf16[64,24,128]{2,1,0:T(8,128)(2,1)S(1)}, bf16[64,24,128]{2,1,0:T(8,128)(2,1)S(1)}, u32[]{:S(2)}, u32[]{:S(2)}) collective-permute-start(bf16[64,24,128]{2,1,0:T(8,128)(2,1)S(1)} %all_to_all.11.g_own), channel_id=1, source_target_pairs={{0,1},{1,0},{2,3},{3,2},{4,5},{5,4},{6,7},{7,6},{8,9},{9,8},{10,11... | collective-permute-start | bytes 1179656 | tf_op jit(solution)/shard_map/ppermute | solution.py:419
  106.9 2.0 %collective-permute-start.5 = (bf16[768,256]{1,0:T(8,128)(2,1)S(1)}, bf16[768,256]{1,0:T(8,128)(2,1)S(1)}, u32[]{:S(2)}, u32[]{:S(2)}) collective-permute-start(bf16[768,256]{1,0:T(8,128)(2,1)S(1)} %get-tuple-element.25.at_own), channel_id=1, source_target_pairs={{0,1},{1,0},{2,3},{3,2},{4,5},{5,4},{6,7},{7,6},{8,9},{9,8},{10,11... | collective-permute-start | bytes 1179656 | tf_op jit(solution)/shard_map/ppermute | solution.py:419
  107.3 1.5 %collective-permute-start.6 = (bf16[256,256]{1,0:T(8,128)(2,1)S(1)}, bf16[256,256]{1,0:T(8,128)(2,1)S(1)}, u32[]{:S(2)}, u32[]{:S(2)}) collective-permute-start(bf16[256,256]{1,0:T(8,128)(2,1)S(1)} %get-tuple-element.26.b_own), channel_id=1, source_target_pairs={{0,1},{1,0},{2,3},{3,2},{4,5},{5,4},{6,7},{7,6},{8,9},{9,8},{10,11... | collective-permute-start | bytes 393224 | tf_op jit(solution)/shard_map/ppermute | solution.py:419
where the time goes:
time: 134 us
  Pallas kernels  79.2 us (59%)
  blocking collectives  38 us (28%)
  starting transfers between devices  6.06 us (5%)
  local copies, waits for them, and re-layouts  5.13 us (4%)
  waiting for transfers between devices  2.76 us (2%)
  other arithmetic  2.09 us (2%)
    pallas_call x1, Pallas kernels, encode(): pl.pallas_call(encode_kernel, out_shape=shape((OWNERS, 32, 128)), in_spec...  37.7 us
    pallas_call x1, Pallas kernels, decode(): pl.pallas_call(decode_kernel, out_shape=shape((16, share), f32), in_specs...  25.1 us
    all_to_all x1, blocking collectives, per_device(): parts = lax.all_to_all(part, 'pts', 0, 0)  23.5 us
    all_to_all x1, blocking collectives, per_device(): g_own = lax.all_to_all(merge(parts, OWNERS), 'pts', 0, 0)  14.5 us
    pallas_call x1, Pallas kernels, latent_block(): pl.pallas_call(latent_kernel, out_shape=(shape((WIDTH, rows)), shape((row...  14.3 us
    ppermute x7, starting transfers between devices, other(): return lax.ppermute(x, 'head', swap)  6.06 us
    unnamed x14, local copies, waits for them, and re-layouts  3.97 us
    ppermute x7, waiting for transfers between devices, other(): return lax.ppermute(x, 'head', swap)  2.76 us
  transfers between devices with their start and end apart: 7, of which 2 were waited for; matrix products, arithmetic and copies ran while one was open for 1% of the time, Pallas kernels for 30%

commit v1 on v0

--- a/solution.py
+++ b/solution.py
@@ -77,7 +77,7 @@
     return pl.CostEstimate(flops=flops, bytes_accessed=size, transcendentals=exps)
 
 
-def prepare_kernel(count_ref, pts_ref, pack_ref, paug, pvt, normed, pn_ref):
+def prepare_kernel(count_ref, pts_ref, pack_ref, before, paug, pvt, normed, pn_ref):
     slots = pts_ref.shape[1]
     count = count_ref[0]
     sub = lax.broadcasted_iota(jnp.int32, (64, slots), 0)
@@ -94,17 +94,17 @@
     pn_ref[0] = jnp.max(jnp.sum(pall * pall, axis=0, keepdims=True))
 
 
-def prepare(count, points, pack):
+def prepare(count, points, pack, before):
     slots = points.shape[1]
     return pl.pallas_call(
         prepare_kernel,
         out_shape=(shape((128, slots)), shape((slots, 128)), shape((pack.shape[0] - HALF, WIDTH)), shape((1,), f32)),
-        in_specs=[smem(), vmem(), vmem()],
+        in_specs=[smem(), vmem(), vmem(), anywhere()],
         out_specs=(vmem(), vmem(), vmem(), smem()),
         compiler_params=params(),
         cost_estimate=cost(0, 6 << 20),
         name="prepare",
-    )(count, points, pack)
+    )(count, points, pack, before)
 
 
 ROW_TILE = 512
@@ -161,13 +161,10 @@
         base = pl.multiple_of(t * ROW_TILE, ROW_TILE)
         qt = qaug[pl.ds(base, ROW_TILE), :]
         total = jnp.zeros((ROW_TILE, 128), f32)
-        chunks = [slice(j * PT_TILE, (j + 1) * PT_TILE) for j in range(slots // PT_TILE)]
-        coming = dot(qt, paug[:, chunks[0]])
-        for j, cols in enumerate(chunks):
-            sc = coming
-            if j + 1 < len(chunks):
-                coming = dot(qt, paug[:, chunks[j + 1]])
-            total = total + dot(jnp.exp2(sc).astype(bf16), pvt[cols, :])
+        for j in range(slots // PT_TILE):
+            cols = slice(j * PT_TILE, (j + 1) * PT_TILE)
+            ex = jnp.exp2(dot(qt, paug[:, cols])).astype(bf16)
+            total = total + dot(ex, pvt[cols, :])
         acc[pl.ds(base, ROW_TILE), :] = total
         return 0
 
@@ -258,11 +255,16 @@
     pos_ref, g_own, g_oth, pack_own, pack_oth, small,
     wl_own, wl_oth, up_own, up_oth, down_own, down_oth,
     at_ref, b_ref,
-    enc, mix,
+    enc, mix, wbuf, sem,
 ):
     rows = mix.shape[0]
     head = pos_ref[0]
-    first = head == 0
+    copies = {}
+    for i in (2, 3, 1, 4, 5, 6):
+        for k, (src, at) in enumerate(((wl_own, head), (wl_oth, 1 - head))):
+            dst = wbuf.at[i - 1, pl.ds(pl.multiple_of(at * HALF, HALF), HALF)]
+            copies[i, k] = pltpu.make_async_copy(src.at[i], dst, sem.at[i - 1, k])
+            copies[i, k].start()
     for k, (g, pack) in enumerate(((g_own, pack_own), (g_oth, pack_oth))):
         mean = g[...].astype(f32).reshape(GROUPS, 2, 3, 8, 128)
         for p in range(PAIRS):
@@ -273,8 +275,9 @@
     block_in = norm(enc[...].astype(f32)).astype(bf16)
 
     def proj(x, i):
-        lo, hi = x[:, :HALF], x[:, HALF:]
-        return dot(jnp.where(first, lo, hi), wl_own[i]) + dot(jnp.where(first, hi, lo), wl_oth[i])
+        for k in range(2):
+            copies[i, k].wait()
+        return dot(x, wbuf[i - 1])
 
     keys = proj(block_in, 2).astype(bf16)
     vals = proj(block_in, 3).astype(bf16)
@@ -317,11 +320,13 @@
     return pl.pallas_call(
         latent_kernel,
         out_shape=(shape((WIDTH, rows)), shape((rows, 256))),
-        in_specs=[smem()] + [vmem()] * 11,
+        in_specs=[smem()] + [vmem()] * 5 + [anywhere()] * 2 + [vmem()] * 4,
         out_specs=(vmem(), vmem()),
         scratch_shapes=[
             pltpu.VMEM((2 * rows, WIDTH), bf16),
             pltpu.VMEM((rows, WIDTH), bf16),
+            pltpu.VMEM((6, WIDTH, WIDTH), bf16),
+            pltpu.SemaphoreType.DMA((6, 2)),
         ],
         compiler_params=params(),
         cost_estimate=cost(6 << 30, 20 << 20, 3 << 20),
@@ -422,7 +427,7 @@
     pack_own = jnp.concatenate([lat_weights[0], latents_init], axis=0)
     pack_oth = other(pack_own)
     small = jnp.concatenate([enc_key_w, enc_val_w, query_w, class_w.T], axis=0)
-    paug, pvt, normed, pn = prepare(counts, points, pack_own)
+    paug, pvt, normed, pn = prepare(counts, points, pack_own, small)
     (pn, pack_oth), late = lax.optimization_barrier(((pn, pack_oth), (lat_weights, up_w, down_w)))
     wl_oth, up_oth, down_oth = [other(w) for w in late]
     part = encode(pos, pn, normed, pack_own, pack_oth, small, paug, pvt)

time: 134 us -> 131 us (0.978)
  Pallas kernels: 79.2 us -> 76.1 us
    pallas_call x1, Pallas kernels: 14.3 us -> 11.9 us  [latent_block(): pl.pallas_call(latent_kernel, out_shape=(shape((WIDTH, rows)), shape((row...]
    unnamed x14 -> x24, local copies, waits for them, and re-layouts: 3.97 us -> 4.41 us
  transfers between devices with their start and end apart: 7 -> 7, of which waited for: 2 -> 2; matrix products, arithmetic and copies ran while one was open for 1% -> 0% of each run, Pallas kernels for 30% -> 30%
where the time goes in v1:
time: 131 us; the launch traced here: 130 us
  Pallas kernels  76.1 us (58%)
  blocking collectives  38 us (29%)
  starting transfers between devices  5.94 us (5%)
  local copies, waits for them, and re-layouts  5.59 us (4%)
  waiting for transfers between devices  2.77 us (2%)
    pallas_call x1, Pallas kernels, encode(): pl.pallas_call(encode_kernel, out_shape=shape((OWNERS, 32, 128)), in_spec...  36.9 us
    pallas_call x1, Pallas kernels, decode(): pl.pallas_call(decode_kernel, out_shape=shape((16, share), f32), in_specs...  25.1 us
    all_to_all x1, blocking collectives, per_device(): parts = lax.all_to_all(part, 'pts', 0, 0)  23.5 us
    all_to_all x1, blocking collectives, per_device(): g_own = lax.all_to_all(merge(parts, OWNERS), 'pts', 0, 0)  14.4 us
    pallas_call x1, Pallas kernels, latent_block(): pl.pallas_call(latent_kernel, out_shape=(shape((WIDTH, rows)), shape((row...  11.9 us
    ppermute x7, starting transfers between devices, other(): return lax.ppermute(x, 'head', swap)  5.94 us
    unnamed x24, local copies, waits for them, and re-layouts  4.41 us
    ppermute x7, waiting for transfers between devices, other(): return lax.ppermute(x, 'head', swap)  2.77 us
  transfers between devices with their start and end apart: 7, of which 2 were waited for; matrix products, arithmetic and copies ran while one was open for 0% of the time, Pallas kernels for 30%

profile of v1, /device:TPU:1, one launch (start us, length us, event | category | flops | bytes accessed | tf_op | source)
XLA Modules:
  0.0 130.2 jit_solution(12647017690743985546)
XLA Ops:
  0.0 0.0 copy-start.10
  0.0 0.0 copy-start
  0.0 1.2 slice_bitcast_fusion
  1.2 1.1 pad_maximum_fusion.pack_ref.pack_own
  2.3 1.5 %collective-permute-start = (bf16[640,768]{1,0:T(8,128)(2,1)S(1)}, bf16[640,768]{1,0:T(8,128)(2,1)S(1)}, u32[]{:S(2)}, u32[]{:S(2)}) collective-permute-start(bf16[640,768]{1,0:T(8,128)(2,1)S(1)} %pad_maximum_fusion.pack_ref.pack_own), channel_id=1, source_target_pairs={{0,1},{1,0},{2,3},{3,2},{4,5},{5,4},{6,7},{7,6},{8,9},{9,8},{10,11... | collective-permute-start | bytes 2949128 | tf_op jit(solution)/shard_map/ppermute | solution.py:424
  4.4 0.0 copy-done.11
  4.5 1.1 prepare.1
  5.6 0.0 copy-start.3
  5.7 1.0 copy-done.3
  6.6 0.0 collective-permute-done.pack_oth
  6.6 1.0 copy-done.5
  7.6 0.0 collective-permute-start.2
  7.6 0.5 collective-permute-start.3
  8.1 0.0 collective-permute-start.4
  8.1 1.2 copy-done.4
  9.4 1.2 copy-done.6
  10.6 36.9 %encode.1 = bf16[64,32,128]{2,1,0:T(8,128)(2,1)S(1)} custom-call(s32[1]{0:T(128)} %bitcast.pos_ref, f32[1]{0:T(128)} %get-tuple-element.17.pn_ref, bf16[256,768]{1,0:T(8,128)(2,1)S(1)} %get-tuple-element.18.normed, bf16[640,768]{1,0:T(8,128)(2,1)S(1)} %pad_maximum_fusion.pack_ref.pack_own, bf16[640,768]{1,0:T(8,128)(2,1)S(1)} %copy-done.6, ...), custom_call_target="tpu_custom_call" | custom-call | flops 12884901888 | bytes 6291456 | tf_op jit(solution)/shard_map/encode/pallas_call | solution.py:198
  47.5 0.0 copy-start.1
  47.5 23.5 %all_to_all.10.x_ref = bf16[64,32,128]{2,1,0:T(8,128)(2,1)S(1)} all-to-all(bf16[64,32,128]{2,1,0:T(8,128)(2,1)S(1)} %encode.1), channel_id=1, replica_groups=mesh['pts'=64,'head'=2] {'pts'}, dimensions={0} | all-to-all | bytes 1048576 | tf_op jit(solution)/shard_map/all_to_all | solution.py:435
  71.0 1.0 merge.1
  72.0 14.4 %all_to_all.11.g_own = bf16[64,24,128]{2,1,0:T(8,128)(2,1)S(1)} all-to-all(bf16[64,24,128]{2,1,0:T(8,128)(2,1)S(1)} %merge.1), channel_id=1, replica_groups=mesh['pts'=64,'head'=2] {'pts'}, dimensions={0} | all-to-all | bytes 786432 | tf_op jit(solution)/shard_map/all_to_all | solution.py:436
  86.4 3.3 %collective-permute-start.1 = (bf16[64,24,128]{2,1,0:T(8,128)(2,1)S(1)}, bf16[64,24,128]{2,1,0:T(8,128)(2,1)S(1)}, u32[]{:S(2)}, u32[]{:S(2)}) collective-permute-start(bf16[64,24,128]{2,1,0:T(8,128)(2,1)S(1)} %all_to_all.11.g_own), channel_id=1, source_target_pairs={{0,1},{1,0},{2,3},{3,2},{4,5},{5,4},{6,7},{7,6},{8,9},{9,8},{10,11... | collective-permute-start | bytes 1179656 | tf_op jit(solution)/shard_map/ppermute | solution.py:424
  89.8 1.3 %collective-permute-done.1.g_oth = bf16[64,24,128]{2,1,0:T(8,128)(2,1)S(1)} collective-permute-done((bf16[64,24,128]{2,1,0:T(8,128)(2,1)S(1)}, bf16[64,24,128]{2,1,0:T(8,128)(2,1)S(1)}, u32[]{:S(2)}, u32[]{:S(2)}) %collective-permute-start.1) | collective-permute-done | bytes 393248 | tf_op jit(solution)/shard_map/ppermute | solution.py:424
  91.1 0.0 collective-permute-done.3.up_oth
  91.1 0.0 collective-permute-done.4.down_oth
  91.1 0.0 collective-permute-done.2.wl_oth
  91.2 11.9 %latent_block.1 = (bf16[768,256]{1,0:T(8,128)(2,1)S(1)}, bf16[256,256]{1,0:T(8,128)(2,1)S(1)}) custom-call(s32[1]{0:T(128)} %bitcast.pos_ref, bf16[64,24,128]{2,1,0:T(8,128)(2,1)S(1)} %all_to_all.11.g_own, bf16[64,24,128]{2,1,0:T(8,128)(2,1)S(1)} %collective-permute-done.1.g_oth, bf16[640,768]{1,0:T(8,128)(2,1)S(1)} %pad_maximum_fusion.pack_ref.pack_own, ...), custom_call_target="tpu_custom_call" | custom-call | flops 6442450944 | bytes 20971520 | tf_op jit(solution)/shard_map/latent_block/pallas_call | solution.py:320
  103.1 0.5 collective-permute-start.5
  103.6 0.1 collective-permute-start.6
  103.7 1.4 %collective-permute-done.6.b_oth = bf16[256,256]{1,0:T(8,128)(2,1)S(1)} collective-permute-done((bf16[256,256]{1,0:T(8,128)(2,1)S(1)}, bf16[256,256]{1,0:T(8,128)(2,1)S(1)}, u32[]{:S(2)}, u32[]{:S(2)}) %collective-permute-start.6) | collective-permute-done | bytes 131104 | tf_op jit(solution)/shard_map/ppermute | solution.py:424
  105.1 0.0 collective-permute-done.5.at_oth
  105.1 25.1 %decode.1 = f32[16,2048]{1,0:T(8,128)} custom-call(s32[1]{0:T(128)} %bitcast.pos_ref, f32[1]{0:T(128)} %get-tuple-element.17.pn_ref, bf16[64,4096]{1,0:T(8,128)(2,1)S(1)} %copy-done, bf16[768,256]{1,0:T(8,128)(2,1)S(1)} %get-tuple-element.25.at_own, bf16[768,256]{1,0:T(8,128)(2,1)S(1)} %collective-permute-done.5.at_oth, ...), custom_call_target="tpu_custom_call" | custom-call | flops 12884901888 | bytes 8388608 | tf_op jit(solution)/shard_map/decode/pallas_call | solution.py:402
  (16 shorter events, 0.1 us)
Async XLA Ops:
  0.0 4.4 %copy-start.11 = (bf16[768,16]{0,1:T(8,128)(2,1)S(1)}, bf16[768,16]{0,1:T(8,128)(2,1)}, u32[]{:S(2)}) copy-start(bf16[768,16]{0,1:T(8,128)(2,1)} %param.19) | copy-start | bytes 73732
  0.0 4.4 %copy-start.8 = (bf16[64,768]{1,0:T(8,128)(2,1)S(1)}, bf16[64,768]{1,0:T(8,128)(2,1)}, u32[]{:S(2)}) copy-start(bf16[64,768]{1,0:T(8,128)(2,1)} %param.18) | copy-start | bytes 294916
  0.0 4.4 %copy-start.9 = (bf16[64,768]{1,0:T(8,128)(2,1)S(1)}, bf16[64,768]{1,0:T(8,128)(2,1)}, u32[]{:S(2)}) copy-start(bf16[64,768]{1,0:T(8,128)(2,1)} %param.14) | copy-start | bytes 294916
  0.0 4.4 %copy-start.10 = (bf16[64,768]{1,0:T(8,128)(2,1)S(1)}, bf16[64,768]{1,0:T(8,128)(2,1)}, u32[]{:S(2)}) copy-start(bf16[64,768]{1,0:T(8,128)(2,1)} %param.13) | copy-start | bytes 294916
  0.0 4.5 %copy-start = (bf16[64,4096]{1,0:T(8,128)(2,1)S(1)}, bf16[64,4096]{1,0:T(8,128)(2,1)}, u32[]{:S(2)}) copy-start(bf16[64,4096]{1,0:T(8,128)(2,1)} %pts_ref.3) | copy-start | bytes 1572868
  2.3 4.4 %collective-permute-start = (bf16[640,768]{1,0:T(8,128)(2,1)S(1)}, bf16[640,768]{1,0:T(8,128)(2,1)S(1)}, u32[]{:S(2)}, u32[]{:S(2)}) collective-permute-start(bf16[640,768]{1,0:T(8,128)(2,1)S(1)} %pad_maximum_fusion.pack_ref.pack_own), channel_id=1, source_target_pairs={{0,1},{1,0},{2,3},{3,2},{4,5},{5,4},{6,7},{7,6},{8,9},{9,8},{10,11... | collective-permute-start | bytes 2949128 | tf_op jit(solution)/shard_map/ppermute | solution.py:424
  5.6 1.0 copy-start.3
  6.6 1.0 copy-start.5
  7.6 83.5 %collective-permute-start.2 = (bf16[7,384,768]{2,1,0:T(8,128)(2,1)}, bf16[7,384,768]{2,1,0:T(8,128)(2,1)}, u32[]{:S(2)}, u32[]{:S(2)}) collective-permute-start(bf16[7,384,768]{2,1,0:T(8,128)(2,1)} %wl_own.1), channel_id=1, source_target_pairs={{0,1},{1,0},{2,3},{3,2},{4,5},{5,4},{6,7},{7,6},{8,9},{9,8},{10,11... | collective-permute-start | bytes 12386312 | tf_op jit(solution)/shard_map/ppermute | solution.py:424
  7.6 83.5 %collective-permute-start.3 = (bf16[768,1536]{1,0:T(8,128)(2,1)}, bf16[768,1536]{1,0:T(8,128)(2,1)S(1)}, u32[]{:S(2)}, u32[]{:S(2)}) collective-permute-start(bf16[768,1536]{1,0:T(8,128)(2,1)} %up_own.1), channel_id=1, source_target_pairs={{0,1},{1,0},{2,3},{3,2},{4,5},{5,4},{6,7},{7,6},{8,9},{9,8},{10,11... | collective-permute-start | bytes 7077896 | tf_op jit(solution)/shard_map/ppermute | solution.py:424
  8.1 83.0 %collective-permute-start.4 = (bf16[1536,768]{1,0:T(8,128)(2,1)}, bf16[1536,768]{1,0:T(8,128)(2,1)S(1)}, u32[]{:S(2)}, u32[]{:S(2)}) collective-permute-start(bf16[1536,768]{1,0:T(8,128)(2,1)} %down_own.1), channel_id=1, source_target_pairs={{0,1},{1,0},{2,3},{3,2},{4,5},{5,4},{6,7},{7,6},{8,9},{9,8},{10,11... | collective-permute-start | bytes 7077896 | tf_op jit(solution)/shard_map/ppermute | solution.py:424
  8.1 1.2 copy-start.4
  9.4 1.2 copy-start.6
  10.6 80.6 %copy-start.2 = (bf16[1536,768]{1,0:T(8,128)(2,1)S(1)}, bf16[1536,768]{1,0:T(8,128)(2,1)}, u32[]{:S(2)}) copy-start(bf16[1536,768]{1,0:T(8,128)(2,1)} %down_own.1) | copy-start | bytes 7077892
  10.6 80.6 %copy-start.7 = (bf16[640,768]{1,0:T(8,128)(2,1)S(1)}, bf16[640,768]{1,0:T(8,128)(2,1)}, u32[]{:S(2)}) copy-start(bf16[640,768]{1,0:T(8,128)(2,1)} %copy-done.5) | copy-start | bytes 2949124
  47.5 43.7 %copy-start.1 = (bf16[768,1536]{1,0:T(8,128)(2,1)S(1)}, bf16[768,1536]{1,0:T(8,128)(2,1)}, u32[]{:S(2)}) copy-start(bf16[768,1536]{1,0:T(8,128)(2,1)} %up_own.1) | copy-start | bytes 7077892
  86.4 4.7 %collective-permute-start.1 = (bf16[64,24,128]{2,1,0:T(8,128)(2,1)S(1)}, bf16[64,24,128]{2,1,0:T(8,128)(2,1)S(1)}, u32[]{:S(2)}, u32[]{:S(2)}) collective-permute-start(bf16[64,24,128]{2,1,0:T(8,128)(2,1)S(1)} %all_to_all.11.g_own), channel_id=1, source_target_pairs={{0,1},{1,0},{2,3},{3,2},{4,5},{5,4},{6,7},{7,6},{8,9},{9,8},{10,11... | collective-permute-start | bytes 1179656 | tf_op jit(solution)/shard_map/ppermute | solution.py:424
  103.1 2.0 %collective-permute-start.5 = (bf16[768,256]{1,0:T(8,128)(2,1)S(1)}, bf16[768,256]{1,0:T(8,128)(2,1)S(1)}, u32[]{:S(2)}, u32[]{:S(2)}) collective-permute-start(bf16[768,256]{1,0:T(8,128)(2,1)S(1)} %get-tuple-element.25.at_own), channel_id=1, source_target_pairs={{0,1},{1,0},{2,3},{3,2},{4,5},{5,4},{6,7},{7,6},{8,9},{9,8},{10,11... | collective-permute-start | bytes 1179656 | tf_op jit(solution)/shard_map/ppermute | solution.py:424
  103.6 1.5 %collective-permute-start.6 = (bf16[256,256]{1,0:T(8,128)(2,1)S(1)}, bf16[256,256]{1,0:T(8,128)(2,1)S(1)}, u32[]{:S(2)}, u32[]{:S(2)}) collective-permute-start(bf16[256,256]{1,0:T(8,128)(2,1)S(1)} %get-tuple-element.26.b_own), channel_id=1, source_target_pairs={{0,1},{1,0},{2,3},{3,2},{4,5},{5,4},{6,7},{7,6},{8,9},{9,8},{10,11... | collective-permute-start | bytes 393224 | tf_op jit(solution)/shard_map/ppermute | solution.py:424
